TPU v7x, 256 devices: a whole 4x4x8 slice. The times are simulated.
256 devices in a mesh: space: 32 (over z_lo, y, core), mem: 8 (over z_hi, x).
Axes of the slice: x: 4, y: 4, z: 8 (z_hi: 2, z_lo: 4; z = z_hi * 4 + z_lo), core: 2. Of those that a mesh axis runs over, the one named last changes fastest.
Arguments:
- control: bfloat16 [56, 8, 1024, 256], P('mem', None, 'space'), may hold values from -6 to 6
- ensemble: bfloat16 [56, 8, 256, 1024], P('mem', None, 'space'), may hold values from -0.75 to 0.75
- innovation: float32 [8, 256, 1024], P(None, 'space'), may hold values from -6 to 6
- precision_obs: float32 [8, 256, 1024], P(None, 'space'), may hold values from 1 to 4
- classes_x: int32 [2], replicated, may hold values from 0 to 7
- classes_y: int32 [8], replicated, may hold values from 0 to 7
- tables_x: bfloat16 [8, 5, 128, 128], replicated, may hold values from -0.5 to 2, as said below
- tables_y: bfloat16 [8, 5, 128, 128], replicated, may hold values from -0.5 to 2, as said below
Outputs:
- increment: float32 [8, 256, 1024], P('mem', 'space')
- gradient: bfloat16 [56, 8, 1024, 256], P('mem', None, 'space')
Inputs may be any that keep to these rules, and one draw needn't show every extreme that they name: `tables_x`: blocks of the banded filter matrices of each scale class. `tables_y`: blocks of the banded filter matrices of each scale class.
All inputs are finite; a program needn't handle non-finite values.
Results may differ from a plain program's by a relative error of at most 0.0056.
Values may be sent and summed in bfloat16 or wider, within the bound.
A program may use at most 64 MiB of HBM per device.

v0:
```python
import jax
import jax.numpy as jnp
from jax import lax
from jax.sharding import PartitionSpec as P


def band_apply(values, tables, classes):
    tile_size = tables.shape[-1]
    band_count = tables.shape[1]
    margin = (band_count - 1) // 2
    leading = values.shape[:-1]
    tile_count = values.shape[-1] // tile_size
    blocks = values.reshape(leading + (tile_count, tile_size))
    padded = jnp.pad(blocks, [(0, 0)] * len(leading) + [(margin, margin), (0, 0)])
    windows = jnp.stack(
        [padded[..., slot_index : slot_index + tile_count, :] for slot_index in range(band_count)],
        axis=-2,
    )
    chosen = tables[classes]
    result = jnp.einsum("...bki,bkij->...bj", windows, chosen, preferred_element_type=jnp.float32)
    return result.reshape(leading + (tile_count * tile_size,))


def band_adjoint(values, tables, classes):
    tile_size = tables.shape[-1]
    band_count = tables.shape[1]
    margin = (band_count - 1) // 2
    leading = values.shape[:-1]
    tile_count = values.shape[-1] // tile_size
    blocks = values.reshape(leading + (tile_count, tile_size))
    chosen = tables[classes]
    pieces = jnp.einsum("...bj,bkij->...bki", blocks, chosen, preferred_element_type=jnp.float32)
    padded = jnp.pad(pieces, [(0, 0)] * len(leading) + [(margin, margin), (0, 0), (0, 0)])
    result = jnp.zeros(leading + (tile_count, tile_size), jnp.float32)
    for slot_index in range(band_count):
        begin = 2 * margin - slot_index
        result = result + padded[..., begin : begin + tile_count, slot_index, :]
    return result.reshape(leading + (tile_count * tile_size,))


def to_columns(values, pieces):
    members, levels, row_count, extent = values.shape
    col_count = extent // pieces
    shaped = values.reshape(members, levels, row_count, pieces, col_count)
    return shaped.transpose(0, 1, 3, 4, 2).reshape(members, levels, pieces, col_count * row_count)


def from_rows(received, col_count):
    members, levels, pieces, flat_size = received.shape
    row_count = flat_size // col_count
    shaped = received.reshape(members, levels, pieces, col_count, row_count)
    return shaped.transpose(0, 1, 3, 2, 4).reshape(members, levels, col_count, pieces * row_count)


def to_rows(values, pieces):
    members, levels, col_count, extent = values.shape
    row_count = extent // pieces
    shaped = values.reshape(members, levels, col_count, pieces, row_count)
    return shaped.transpose(0, 1, 3, 2, 4).reshape(members, levels, pieces, col_count * row_count)


def from_columns(received, row_count):
    members, levels, pieces, flat_size = received.shape
    col_count = flat_size // row_count
    shaped = received.reshape(members, levels, pieces, col_count, row_count)
    return shaped.transpose(0, 1, 4, 2, 3).reshape(members, levels, row_count, pieces * col_count)


def per_device(
    control, ensemble, innovation, precision_obs, classes_x, classes_y, tables_x, tables_y
):
    pieces = lax.axis_size("space")
    row_count = control.shape[2]
    col_count = ensemble.shape[2]
    levels = control.shape[1]
    level_share = levels // lax.axis_size("mem")
    offset = lax.axis_index("mem") * level_share
    smooth_x = band_apply(control, tables_x, classes_x).astype(jnp.bfloat16)
    packed = to_columns(smooth_x, pieces)
    smooth_y = band_apply(
        from_rows(
            lax.all_to_all(packed, "space", split_axis=2, concat_axis=2, tiled=True), col_count
        ),
        tables_y,
        classes_y,
    )
    partial_sum = jnp.sum(ensemble.astype(jnp.float32) * smooth_y, axis=0)
    summed = lax.psum(partial_sum, "mem")
    increment = lax.dynamic_slice_in_dim(summed, offset, level_share, 0)
    weighted_res = precision_obs * (summed - innovation)
    member_force = (ensemble.astype(jnp.float32) * weighted_res).astype(jnp.bfloat16)
    back_y = band_adjoint(member_force, tables_y, classes_y).astype(jnp.bfloat16)
    back_x = band_adjoint(
        from_columns(
            lax.all_to_all(
                to_rows(back_y, pieces), "space", split_axis=2, concat_axis=2, tiled=True
            ),
            row_count,
        ),
        tables_x,
        classes_x,
    )
    gradient = (control.astype(jnp.float32) + back_x).astype(jnp.bfloat16)
    return (increment, gradient)


def solution(mesh):
    in_specs = (
        P("mem", None, "space", None),
        P("mem", None, "space", None),
        P(None, "space", None),
        P(None, "space", None),
        P(),
        P(),
        P(),
        P(),
    )
    out_specs = (P("mem", "space", None), P("mem", None, "space", None))
    return jax.shard_map(
        per_device, mesh=mesh, in_specs=in_specs, out_specs=out_specs, check_vma=False
    )
```

profile of v0, /device:TPU:1, one launch (start us, length us, event | category | flops | bytes accessed | tf_op | source)
XLA Modules:
  0.0 267.5 jit_solution(1403302008026371591)
XLA Ops:
  7.2 1.5 copy_bitcast_fusion.1
  8.7 2.2 stack.36
  10.9 0.2 broadcast_dynamic-update-slice_fusion
  11.1 0.2 fusion.27
  11.3 0.3 copy_dynamic-update-slice_fusion.1
  11.6 0.2 fusion.29
  11.8 0.3 broadcast_dynamic-update-slice_fusion.1
  12.0 2.1 copy-done.8
  14.1 1.9 gather_fusion.1
  16.1 3.7 %fusion.14 = bf16[7,8,32,2,128]{4,2,1,0,3:T(8,128)(2,1)S(1)} fusion(bf16[7,8,32,2,5,128]{5,2,4,1,0,3:T(8,128)(2,1)} %copy-done.8, bf16[2,5,128,128]{3,2,1,0:T(8,128)(2,1)S(1)} %gather_fusion.1), kind=kOutput, calls=%fused_computation.33 | convolution fusion | flops 587661312 | bytes 5832704 | tf_op jit(solution)/shard_map/...bki,bkij->...bj/dot_general | solution.py:20
  19.8 2.9 %copy.34 = bf16[7,8,32,2,128]{2,4,3,1,0:T(8,128)(2,1)} copy(bf16[7,8,32,2,128]{4,2,1,0,3:T(8,128)(2,1)S(1)} %fusion.14) | data formatting | bytes 1835008 | tf_op jit(solution)/shard_map/convert_element_type | solution.py:78
  22.7 4.8 %reshape.56 = bf16[7,8,32,256]{3,2,1,0:T(8,128)(2,1)S(1)} reshape(bf16[7,8,32,8,32]{4,3,2,1,0:T(8,128)(2,1)} %bitcast.124) | data formatting | bytes 1835008 | tf_op jit(solution)/shard_map/reshape | solution.py:45
  27.5 1.4 copy.35
  29.0 10.2 %all-to-all-start = ((bf16[7,8,32,256]{3,1,0,2:T(8,128)(2,1)}), bf16[7,8,32,256]{3,1,0,2:T(8,128)(2,1)S(1)}, u32[]{:S(2)}, u32[]{:S(2)}) async-start(bf16[7,8,32,256]{3,1,0,2:T(8,128)(2,1)} %copy.35), calls=%async_computation | async-start | bytes 1835008 | tf_op jit(solution)/shard_map/all_to_all | solution.py:82
  39.2 0.2 all-reduce.6.cloned.1.call-start
  39.4 0.8 gather_fusion
  40.2 23.0 %all-to-all-done = bf16[7,8,32,256]{3,1,0,2:T(8,128)(2,1)S(1)} async-done(((bf16[7,8,32,256]{3,1,0,2:T(8,128)(2,1)}), bf16[7,8,32,256]{3,1,0,2:T(8,128)(2,1)S(1)}, u32[]{:S(2)}, u32[]{:S(2)}) %all-to-all-start) | async-done | bytes 917536 | tf_op jit(solution)/shard_map/all_to_all | solution.py:82
  63.2 3.1 %reshape.57 = bf16[7,8,32,8,32]{4,3,1,0,2:T(8,128)(2,1)} reshape(bf16[7,8,32,256]{3,1,0,2:T(8,128)(2,1)S(1)} %all-to-all-done) | data formatting | bytes 1835008 | tf_op jit(solution)/shard_map/reshape | solution.py:51
  66.2 8.1 %copy.77 = bf16[7,8,32,8,32]{4,2,3,1,0:T(8,128)(2,1)} copy(bf16[7,8,32,8,32]{4,3,1,0,2:T(8,128)(2,1)} %reshape.57) | data formatting | bytes 1835008 | tf_op jit(solution)/shard_map/reshape | solution.py:51
  74.4 4.7 %stack.41 = bf16[7,8,8,8,1,128]{5,3,2,1,0,4:T(8,128)(2,1)S(1)} reshape(bf16[7,8,8,32,32]{4,3,2,1,0:T(8,128)(2,1)} %bitcast.120) | data formatting | bytes 1835008 | tf_op jit(solution)/shard_map/stack | solution.py:15
  79.0 5.5 %reshape_reshape.6 = bf16[7,8,8,8,128]{4,3,2,1,0:T(8,128)(2,1)} reshape(bf16[7,8,8,32,32]{4,3,2,1,0:T(8,128)(2,1)} %bitcast.121) | data formatting | bytes 1835008 | tf_op jit(solution)/shard_map/reshape;reshape | solution.py:13
  84.5 1.4 copy.37
  85.9 0.2 fusion.18
  86.1 0.3 fusion.20
  86.4 0.4 copy_dynamic-update-slice_fusion
  86.7 0.3 fusion.22
  87.0 0.3 fusion.24
  87.4 1.3 convolution_bitcast_fusion.1
  88.7 0.9 fusion.5
  89.7 0.0 all-reduce.6.cloned.1.call-update
  89.7 100.5 %all-reduce.6.cloned.1.call-done = f32[8,8,1024]{2,1,0:T(8,128)} async-done(((f32[8,8,1024]{2,1,0:T(8,128)}), f32[8,8,1024]{2,1,0:T(8,128)}) %all-reduce.6.cloned.1.call-update) | async-done | bytes 262160 | tf_op jit(solution)/shard_map/psum | solution.py:88
  190.2 1.0 subtract_multiply_fusion
  191.2 1.4 convolution_bitcast_fusion
  192.6 0.9 fusion.11
  193.5 1.1 copy.44
  194.6 3.0 %add.73 = bf16[7,8,8,32,32]{4,3,2,1,0:T(8,128)(2,1)} reshape(bf16[7,8,8,8,1,128]{5,3,2,1,0,4:T(8,128)(2,1)S(1)} %copy.44) | data formatting | bytes 1835008 | tf_op jit(solution)/shard_map/add | solution.py:37
  197.6 5.3 %copy.60 = bf16[7,8,32,8,32]{4,3,1,0,2:T(8,128)(2,1)} copy(bf16[7,8,32,8,32]{4,2,3,1,0:T(8,128)(2,1)} %bitcast.123) | data formatting | bytes 1835008 | tf_op jit(solution)/shard_map/reshape | solution.py:59
  202.9 5.6 %reshape.86 = bf16[7,8,32,256]{3,1,0,2:T(8,128)(2,1)} reshape(bf16[7,8,32,8,32]{4,3,1,0,2:T(8,128)(2,1)} %copy.60) | data formatting | bytes 1835008 | tf_op jit(solution)/shard_map/reshape | solution.py:59
  208.5 10.8 %all-to-all-start.1 = ((bf16[7,8,32,256]{3,1,0,2:T(8,128)(2,1)}), bf16[7,8,32,256]{3,1,0,2:T(8,128)(2,1)S(1)}, u32[]{:S(2)}, u32[]{:S(2)}) async-start(bf16[7,8,32,256]{3,1,0,2:T(8,128)(2,1)} %reshape.86), calls=%async_computation.1 | async-start | bytes 1835008 | tf_op jit(solution)/shard_map/all_to_all | solution.py:95
  219.3 1.4 constant_dynamic-slice_fusion
  220.7 22.6 %all-to-all-done.1 = bf16[7,8,32,256]{3,1,0,2:T(8,128)(2,1)S(1)} async-done(((bf16[7,8,32,256]{3,1,0,2:T(8,128)(2,1)}), bf16[7,8,32,256]{3,1,0,2:T(8,128)(2,1)S(1)}, u32[]{:S(2)}, u32[]{:S(2)}) %all-to-all-start.1) | async-done | bytes 917536 | tf_op jit(solution)/shard_map/all_to_all | solution.py:95
  243.3 3.1 %reshape.61 = bf16[7,8,32,8,32]{4,3,1,0,2:T(8,128)(2,1)} reshape(bf16[7,8,32,256]{3,1,0,2:T(8,128)(2,1)S(1)} %all-to-all-done.1) | data formatting | bytes 1835008 | tf_op jit(solution)/shard_map/reshape | solution.py:65
  246.4 3.1 %copy.47 = bf16[7,8,32,8,32]{4,3,2,1,0:T(8,128)(2,1)S(1)} copy(bf16[7,8,32,8,32]{4,3,1,0,2:T(8,128)(2,1)} %reshape.61) | data formatting | bytes 1835008 | tf_op jit(solution)/shard_map/reshape | solution.py:65
  249.5 1.4 fusion.2
  250.9 0.4 fusion.13
  251.3 2.9 %copy.49 = f32[7,8,32,2,1,128]{5,3,2,1,0,4:T(2,128)} copy(f32[7,8,32,2,1,128]{5,2,1,0,4,3:T(8,128)S(1)} %fusion.13) | data formatting | bytes 3670016 | tf_op jit(solution)/shard_map/add | solution.py:37
  254.3 3.6 %add.76 = f32[7,8,32,256]{3,2,1,0:T(8,128)} reshape(f32[7,8,32,2,1,128]{5,3,2,1,0,4:T(2,128)} %copy.49) | data formatting | bytes 3670016 | tf_op jit(solution)/shard_map/add | solution.py:37
  257.9 2.7 %add_convert_fusion = bf16[7,8,32,256]{3,2,1,0:T(8,128)(2,1)} fusion(f32[7,8,32,256]{3,2,1,0:T(8,128)} %add.76, bf16[7,8,32,256]{3,2,1,0:T(8,128)(2,1)S(1)} %copy-done.2), kind=kLoop, calls=%fused_computation.27 | loop fusion | flops 1376256 | bytes 3670016 | tf_op jit(solution)/shard_map/convert_element_type | solution.py:103
  (24 shorter events, 0.1 us)
Async XLA Ops:
  7.2 32.2 %copy-start = (bf16[8,5,128,128]{3,2,1,0:T(8,128)(2,1)S(1)}, bf16[8,5,128,128]{3,2,1,0:T(8,128)(2,1)}, u32[]{:S(2)}) copy-start(bf16[8,5,128,128]{3,2,1,0:T(8,128)(2,1)} %param.15) | copy-start | bytes 3932164
  7.2 3.9 %copy-start.9 = (s32[2]{0:T(128)S(1)}, s32[2]{0:T(128)}, u32[]{:S(2)}) copy-start(s32[2]{0:T(128)} %param.12) | copy-start | bytes 28
  7.2 3.9 %copy-start.10 = (s32[8]{0:T(128)S(1)}, s32[8]{0:T(128)}, u32[]{:S(2)}) copy-start(s32[8]{0:T(128)} %param.13) | copy-start | bytes 100
  12.0 2.1 copy-start.8
  16.1 3.8 %copy-start.4 = (bf16[2,5,128,128]{3,2,1,0:T(8,128)(2,1)}, bf16[2,5,128,128]{3,2,1,0:T(8,128)(2,1)S(1)}, u32[]{:S(2)}) copy-start(bf16[2,5,128,128]{3,2,1,0:T(8,128)(2,1)S(1)} %gather_fusion.1) | copy-start | bytes 983044
  29.0 34.2 %all-to-all-start = ((bf16[7,8,32,256]{3,1,0,2:T(8,128)(2,1)}), bf16[7,8,32,256]{3,1,0,2:T(8,128)(2,1)S(1)}, u32[]{:S(2)}, u32[]{:S(2)}) async-start(bf16[7,8,32,256]{3,1,0,2:T(8,128)(2,1)} %copy.35), calls=%async_computation | async-start | bytes 1835008 | tf_op jit(solution)/shard_map/all_to_all | solution.py:82
  39.2 151.1 %all-reduce.6.cloned.1.call-start = ((), (), s32[]{:S(2)}) async-start(), calls=%async_computation.2 | async-start | bytes 524288 | tf_op jit(solution)/shard_map/psum | solution.py:88
  87.3 1.4 copy-start.3
  87.3 102.9 %copy-start.6 = (f32[8,8,1024]{2,1,0:T(8,128)S(1)}, f32[8,8,1024]{2,1,0:T(8,128)}, u32[]{:S(2)}) copy-start(f32[8,8,1024]{2,1,0:T(8,128)} %param.11) | copy-start | bytes 786436
  87.3 102.9 %copy-start.7 = (f32[8,8,1024]{2,1,0:T(8,128)S(1)}, f32[8,8,1024]{2,1,0:T(8,128)}, u32[]{:S(2)}) copy-start(f32[8,8,1024]{2,1,0:T(8,128)} %param.10) | copy-start | bytes 786436
  208.5 34.8 %all-to-all-start.1 = ((bf16[7,8,32,256]{3,1,0,2:T(8,128)(2,1)}), bf16[7,8,32,256]{3,1,0,2:T(8,128)(2,1)S(1)}, u32[]{:S(2)}, u32[]{:S(2)}) async-start(bf16[7,8,32,256]{3,1,0,2:T(8,128)(2,1)} %reshape.86), calls=%async_computation.1 | async-start | bytes 1835008 | tf_op jit(solution)/shard_map/all_to_all | solution.py:95
  246.4 3.1 %copy-start.5 = (bf16[2,5,128,128]{3,2,1,0:T(8,128)(2,1)S(1)}, bf16[2,5,128,128]{3,2,1,0:T(8,128)(2,1)}, u32[]{:S(2)}) copy-start(bf16[2,5,128,128]{3,2,1,0:T(8,128)(2,1)} %copy-done.4) | copy-start | bytes 983044
  251.3 6.6 %copy-start.2 = (bf16[7,8,32,256]{3,2,1,0:T(8,128)(2,1)S(1)}, bf16[7,8,32,256]{3,2,1,0:T(8,128)(2,1)}, u32[]{:S(2)}) copy-start(bf16[7,8,32,256]{3,2,1,0:T(8,128)(2,1)} %param.8) | copy-start | bytes 2752516
  251.3 9.3 %copy-start.1 = (bf16[8,5,128,128]{3,2,1,0:T(8,128)(2,1)S(1)}, bf16[8,5,128,128]{3,2,1,0:T(8,128)(2,1)}, u32[]{:S(2)}) copy-start(bf16[8,5,128,128]{3,2,1,0:T(8,128)(2,1)} %param.15) | copy-start | bytes 3932164
Sparse Core Ops, SparseCore 0:
  89.8 100.3 all-reduce.5
where the time goes:
time: 269 us; the launch traced here: 267 us
  waiting for transfers between devices  146 us (54%)
  local copies, waits for them, and re-layouts  71.8 us (27%)
  starting transfers between devices  21.2 us (8%)
  between operations  14.4 us (5%)
  matrix products  7.86 us (3%)
  other arithmetic  6 us (2%)
    psum x1, waiting for transfers between devices, per_device(): summed = lax.psum(partial_sum, 'mem')  101 us
    all_to_all x1, waiting for transfers between devices, per_device(): lax.all_to_all(packed, 'space', split_axis=2, concat_axis=2, tiled=True)  23 us
    all_to_all x1, waiting for transfers between devices, per_device(): lax.all_to_all(to_rows(back_y, pieces), 'space', split_axis=2, concat_axi...  22.6 us
    reshape x2, local copies, waits for them, and re-layouts, from_rows(): shaped = received.reshape(members, levels, pieces, col_count, row_count)  11.2 us
    reshape x2, local copies, waits for them, and re-layouts, to_rows(): shaped.transpose(0, 1, 3, 2, 4)  10.9 us
    all_to_all x1, starting transfers between devices, per_device(): lax.all_to_all(to_rows(back_y, pieces), 'space', split_axis=2, concat_axi...  10.8 us
    all_to_all x1, starting transfers between devices, per_device(): lax.all_to_all(packed, 'space', split_axis=2, concat_axis=2, tiled=True)  10.2 us
    add x3, local copies, waits for them, and re-layouts, band_adjoint(): result = result + padded[..., begin:begin + tile_count, slot_index, :]  9.58 us
  transfers between devices with their start and end apart: 3, of which 3 were waited for; matrix products, arithmetic and copies ran while one was open for 1% of the time, Pallas kernels for 0%

commit v1 on v0

v1 whole, which is shorter than its diff:
```python
import jax
import jax.numpy as jnp
from jax import lax
from jax.experimental import pallas as pl
from jax.experimental.pallas import tpu as pltpu
from jax.sharding import PartitionSpec as P

MESH = pl.DeviceIdType.MESH
F32 = jnp.float32
BF16 = jnp.bfloat16
NT = (((1,), (1,)), ((), ()))
TN = (((0,), (0,)), ((), ()))

SPACE = 32
MEM = 8
XS = 4
M = 7
LEVELS = 8
CHUNKS = 2
LC = LEVELS // CHUNKS
ROWS = 32
COLS = 8
NX = 256
NY = 1024
B = 128
NB = NY // B
LANES = M * LC * ROWS


def swap_groups(tiles):
    a, b, c, d = tiles
    axis = a.ndim - 1
    lane = lax.broadcasted_iota(jnp.int32, a.shape, axis)
    low = lane < 64
    even = lax.rem(lane, 64) < 32

    def far(p, q):
        return jnp.where(low, p, pltpu.roll(q, 64, axis)), jnp.where(low, pltpu.roll(p, 64, axis), q)

    def near(p, q):
        return jnp.where(even, p, pltpu.roll(q, 32, axis)), jnp.where(even, pltpu.roll(p, 96, axis), q)

    a, c = far(a, c)
    b, d = far(b, d)
    a, b = near(a, b)
    c, d = near(c, d)
    return a, b, c, d


def kernel(
    classes_x, classes_y, control, ensemble, innovation, precision, tables_x, tables_y,
    increment, gradient,
    ctl, ens, inn, prec, tx, ty, wxt, wy, send1, recv1, send2, recv2, field, part, rs_recv, zsend, zrecv,
    wres, inc, grad,
    in_sem, out_sem, s1_sem, r1_sem, s2_sem, r2_sem, xs_sem, xr_sem, zs_sem, zr_sem, ws_sem, wr_sem,
):
    me = lax.axis_index("space")
    mem = lax.axis_index("mem")
    my_x = lax.rem(mem, XS)
    my_hi = mem // XS
    base = my_hi * XS

    def lv(c):
        return pl.ds(c * LC, LC)

    loads = {
        "ctl0": pltpu.make_async_copy(control.at[:, lv(0)], ctl.at[:, lv(0)], in_sem.at[0]),
        "tx": pltpu.make_async_copy(tables_x, tx, in_sem.at[1]),
        "ctl1": pltpu.make_async_copy(control.at[:, lv(1)], ctl.at[:, lv(1)], in_sem.at[2]),
        "ty": pltpu.make_async_copy(tables_y, ty, in_sem.at[3]),
        "ens": pltpu.make_async_copy(ensemble, ens, in_sem.at[4]),
        "inn0": pltpu.make_async_copy(innovation.at[my_x], inn.at[0], in_sem.at[5]),
        "inn1": pltpu.make_async_copy(innovation.at[LC + my_x], inn.at[1], in_sem.at[6]),
        "prec0": pltpu.make_async_copy(precision.at[my_x], prec.at[0], in_sem.at[7]),
        "prec1": pltpu.make_async_copy(precision.at[LC + my_x], prec.at[1], in_sem.at[8]),
    }
    for copy in loads.values():
        copy.start()

    barrier = pltpu.get_barrier_semaphore()

    @pl.loop(1, SPACE)
    def _(k):
        pl.semaphore_signal(barrier, inc=1, device_id={"space": lax.rem(me + k, SPACE)}, device_id_type=MESH)

    def x_peer(k):
        return lax.rem(my_x + k, XS)

    for k in range(1, XS):
        pl.semaphore_signal(barrier, inc=1, device_id={"mem": base + x_peer(k)}, device_id_type=MESH)
    other_half = lax.rem(mem + XS, MEM)
    pl.semaphore_signal(barrier, inc=1, device_id={"mem": other_half}, device_id_type=MESH)

    loads["tx"].wait()
    for b in range(2):
        for j in range(2):
            block = tx[classes_x[b], j - b + 2]
            wxt[b * B : (b + 1) * B, j * B : (j + 1) * B] = block.astype(F32).T.astype(BF16)

    def x_filter(c):
        for m in range(M):
            rows = ctl[m, c * LC : (c + 1) * LC].reshape(LC * ROWS, NX)
            out = lax.dot_general(wxt[...], rows, NT, preferred_element_type=F32)
            send1[c, :, :, m * B : (m + 1) * B] = out.reshape(SPACE, COLS, B).astype(BF16)

    def space_copy(send, recv, s_sem, r_sem, c, d):
        return pltpu.make_async_remote_copy(
            src_ref=send.at[c, d], dst_ref=recv.at[c, me], send_sem=s_sem.at[c], recv_sem=r_sem.at[c],
            device_id={"space": d}, device_id_type=MESH,
        )

    def all_wait(send, recv, sem, c):
        pltpu.make_async_copy(send.at[c, pl.ds(0, SPACE - 1)], recv.at[c, pl.ds(0, SPACE - 1)], sem.at[c]).wait()

    def start_all(send, recv, s_sem, r_sem, c):
        @pl.loop(1, SPACE)
        def _(k):
            space_copy(send, recv, s_sem, r_sem, c, lax.rem(me + k, SPACE)).start()

        recv[c, me] = send[c, me]

    loads["ctl0"].wait()
    x_filter(0)
    pl.semaphore_wait(barrier, SPACE + XS - 1)
    start_all(send1, recv1, s1_sem, r1_sem, 0)
    loads["ctl1"].wait()
    x_filter(1)

    loads["ty"].wait()
    for b in range(NB):
        for j in range(NB):
            if abs(j - b) <= 2:
                wy[j * B : (j + 1) * B, b * B : (b + 1) * B] = ty[classes_y[b], j - b + 2]
            elif abs(j - b) == 3:
                wy[j * B : (j + 1) * B, b * B : (b + 1) * B] = jnp.zeros((B, B), BF16)

    def band(s):
        return max(0, 2 * s - 2) * B, min(NB, 2 * s + 4) * B

    loads["ens"].wait()
    for name in ("inn0", "inn1", "prec0", "prec1"):
        loads[name].wait()
    all_wait(send1, recv1, s1_sem, 0)
    start_all(send1, recv1, s1_sem, r1_sem, 1)

    def to_fields(c):
        for m in range(M):
            block = recv1[c, :, :, m * B : (m + 1) * B].astype(F32).reshape(NB, 4, COLS, B)
            out = swap_groups([block[:, j] for j in range(4)])
            for b in range(NB):
                tile = jnp.concatenate([out[i][b] for i in range(4)], axis=0)
                field[m * 32 : (m + 1) * 32, b * B : (b + 1) * B] = tile.astype(BF16)

    def members(c, m, lo, hi):
        return ens[m, c * LC : (c + 1) * LC, :, lo:hi].astype(F32).reshape(LC * COLS, hi - lo)

    def forward(c):
        to_fields(c)
        for s in range(NB // 2):
            lo, hi = band(s)
            left, right = 2 * s * B, 2 * (s + 1) * B
            out = jnp.dot(field[:, lo:hi], wy[lo:hi, left:right], preferred_element_type=F32)
            total = jnp.zeros((LC * COLS, 2 * B), F32)
            for m in range(M):
                total = total + members(c, m, left, right) * out[m * 32 : (m + 1) * 32]
            part[c, :, :, left:right] = total.reshape(LC, COLS, 2 * B)

    def reduce(c):
        copies = []
        for k in range(1, XS):
            p = x_peer(k)
            copies.append(pltpu.make_async_remote_copy(
                src_ref=part.at[c, p], dst_ref=rs_recv.at[c, my_x], send_sem=xs_sem.at[c], recv_sem=xr_sem.at[c],
                device_id={"mem": base + p}, device_id_type=MESH,
            ))
        for copy in copies:
            copy.start()
        rs_recv[c, my_x] = part[c, my_x]
        pltpu.make_async_copy(part.at[c, pl.ds(0, XS - 1)], rs_recv.at[c, pl.ds(0, XS - 1)], xr_sem.at[c]).wait()
        zsend[c] = (rs_recv[c, 0] + rs_recv[c, 1]) + (rs_recv[c, 2] + rs_recv[c, 3])
        copy = pltpu.make_async_remote_copy(
            src_ref=zsend.at[c], dst_ref=zrecv.at[c], send_sem=zs_sem.at[c], recv_sem=zr_sem.at[c],
            device_id={"mem": other_half}, device_id_type=MESH,
        )
        copy.start()
        pltpu.make_async_copy(part.at[c, pl.ds(0, XS - 1)], rs_recv.at[c, pl.ds(0, XS - 1)], xs_sem.at[c]).wait()
        copy.wait()
        total = zsend[c] + zrecv[c]

        @pl.when(my_hi == c)
        def _():
            inc[0] = total

        wres[c, my_x] = (prec[c] * (total - inn[c])).astype(BF16)
        copies = []
        for k in range(1, XS):
            copies.append(pltpu.make_async_remote_copy(
                src_ref=wres.at[c, my_x], dst_ref=wres.at[c, my_x], send_sem=ws_sem.at[c], recv_sem=wr_sem.at[c],
                device_id={"mem": base + x_peer(k)}, device_id_type=MESH,
            ))
        for copy in copies:
            copy.start()
        for sem in (ws_sem, wr_sem):
            pltpu.make_async_copy(wres.at[c, pl.ds(0, XS - 1)], wres.at[c, pl.ds(0, XS - 1)], sem.at[c]).wait()

    def backward(c):
        weight = wres[c].astype(F32).reshape(LC * COLS, NY)
        for m in range(M):
            field[m * 32 : (m + 1) * 32] = (members(c, m, 0, NY) * weight).astype(BF16)
        for s in range(NB // 2):
            lo, hi = band(s)
            out = lax.dot_general(
                field[:, lo:hi], wy[2 * s * B : 2 * (s + 1) * B, lo:hi], NT, preferred_element_type=F32
            )
            for half in range(2):
                for m in range(M):
                    rows = out[m * 32 : (m + 1) * 32, half * B : (half + 1) * B].reshape(LC, COLS, B)
                    tiles = swap_groups([rows[i] for i in range(4)])
                    for j in range(4):
                        send2[c, 8 * s + 4 * half + j, :, m * B : (m + 1) * B] = tiles[j].astype(BF16)

    def out_copy(c):
        return pltpu.make_async_copy(grad.at[:, lv(c)], gradient.at[:, lv(c)], out_sem.at[c])

    def finish(c):
        for m in range(M):
            cols = recv2[c, :, :, m * B : (m + 1) * B].astype(F32).reshape(NX, B).astype(BF16)
            out = lax.dot_general(cols, wxt[...], TN, preferred_element_type=F32)
            base_rows = ctl[m, c * LC : (c + 1) * LC].astype(F32)
            grad[m, c * LC : (c + 1) * LC] = (base_rows + out.reshape(LC, ROWS, NX)).astype(BF16)
        out_copy(c).start()

    all_wait(send1, recv1, r1_sem, 0)
    forward(0)
    reduce(0)
    backward(0)
    all_wait(send1, recv1, s1_sem, 1)
    start_all(send2, recv2, s2_sem, r2_sem, 0)
    all_wait(send1, recv1, r1_sem, 1)
    forward(1)
    reduce(1)
    inc_copy = pltpu.make_async_copy(inc, increment, out_sem.at[2])
    inc_copy.start()
    backward(1)
    all_wait(send2, recv2, s2_sem, 0)
    start_all(send2, recv2, s2_sem, r2_sem, 1)
    all_wait(send2, recv2, r2_sem, 0)
    finish(0)
    all_wait(send2, recv2, s2_sem, 1)
    all_wait(send2, recv2, r2_sem, 1)
    finish(1)
    inc_copy.wait()
    out_copy(0).wait()
    out_copy(1).wait()


def per_device(control, ensemble, innovation, precision_obs, classes_x, classes_y, tables_x, tables_y):
    any_space = pl.BlockSpec(memory_space=pl.ANY)
    smem = pl.BlockSpec(memory_space=pltpu.SMEM)
    dma = pltpu.SemaphoreType.DMA
    message = pltpu.VMEM((CHUNKS, SPACE, COLS, LANES), BF16)
    return pl.pallas_call(
        kernel,
        out_shape=(
            jax.ShapeDtypeStruct((1, COLS, NY), F32),
            jax.ShapeDtypeStruct((M, LEVELS, ROWS, NX), BF16),
        ),
        in_specs=[smem, smem] + [any_space] * 6,
        out_specs=(any_space, any_space),
        scratch_shapes=[
            pltpu.VMEM((M, LEVELS, ROWS, NX), BF16),
            pltpu.VMEM((M, LEVELS, COLS, NY), BF16),
            pltpu.VMEM((CHUNKS, COLS, NY), F32),
            pltpu.VMEM((CHUNKS, COLS, NY), F32),
            pltpu.VMEM(tables_x.shape, BF16),
            pltpu.VMEM(tables_y.shape, BF16),
            pltpu.VMEM((NX, NX), BF16),
            pltpu.VMEM((NY, NY), BF16),
            message, message, message, message,
            pltpu.VMEM((M * LC * COLS, NY), BF16),
            pltpu.VMEM((CHUNKS, LC, COLS, NY), F32),
            pltpu.VMEM((CHUNKS, XS, COLS, NY), F32),
            pltpu.VMEM((CHUNKS, COLS, NY), F32),
            pltpu.VMEM((CHUNKS, COLS, NY), F32),
            pltpu.VMEM((CHUNKS, XS, COLS, NY), BF16),
            pltpu.VMEM((1, COLS, NY), F32),
            pltpu.VMEM((M, LEVELS, ROWS, NX), BF16),
            dma((9,)), dma((3,)),
        ] + [dma((CHUNKS,))] * 10,
        compiler_params=pltpu.CompilerParams(
            collective_id=0, has_side_effects=True, vmem_limit_bytes=63 << 20
        ),
        name="hybrid_envar",
    )(classes_x, classes_y, control, ensemble, innovation, precision_obs, tables_x, tables_y)


def solution(mesh):
    in_specs = (
        P("mem", None, "space", None),
        P("mem", None, "space", None),
        P(None, "space", None),
        P(None, "space", None),
        P(),
        P(),
        P(),
        P(),
    )
    out_specs = (P("mem", "space", None), P("mem", None, "space", None))
    return jax.shard_map(
        per_device, mesh=mesh, in_specs=in_specs, out_specs=out_specs, check_vma=False
    )
```

time: 269 us -> 70.4 us (0.26)
  waiting for transfers between devices: 146 us -> 0 us
  local copies, waits for them, and re-layouts: 71.8 us -> 3.56 us
  Pallas kernels: 0 us -> 66 us
  starting transfers between devices: 21.2 us -> 0 us
  between operations: 14.4 us -> 0.64 us
  matrix products: 7.86 us -> 0 us
  other arithmetic: 6 us -> 0 us
    psum x1 -> x0, waiting for transfers between devices: 101 us -> none  [per_device(): summed = lax.psum(partial_sum, 'mem')]
    pallas_call x0 -> x1, Pallas kernels: none -> 66 us  [per_device(): pl.pallas_call(kernel, out_shape=(jax.ShapeDtypeStruct((1, COLS, NY), F32...]
    all_to_all x2 -> x0, waiting for transfers between devices: 45.6 us -> none  [the longest x1 23 us: per_device(): lax.all_to_all(packed, 'space', split_axis=2, concat_axis=2, tiled=True)]
    reshape x9 -> x0, local copies, waits for them, and re-layouts: 35.9 us -> none  [the longest x2 11.2 us: from_rows(): shaped = received.reshape(members, levels, pieces, col_count, row_count)]
    all_to_all x2 -> x0, starting transfers between devices: 21 us -> none  [the longest x1 10.8 us: per_device(): lax.all_to_all(to_rows(back_y, pieces), 'space', split_axis=2, concat_axi...]
    another operation x7 -> x0, local copies, waits for them, and re-layouts: 15.3 us -> none  [the longest x4 7.36 us: band_apply(): jnp.stack([padded[..., slot_index:slot_index + tile_count, :] for slot_in...]
    add x3 -> x0, local copies, waits for them, and re-layouts: 9.58 us -> none  [band_adjoint(): result = result + padded[..., begin:begin + tile_count, slot_index, :]]
    dot_general x4 -> x0, matrix products: 7.86 us -> none  [the longest x2 5.09 us: band_apply(): jnp.einsum('...bki,bkij->...bj', windows, chosen, preferred_element_type=...]
  transfers between devices with their start and end apart: 3 -> 0, of which waited for: 3 -> 0; matrix products, arithmetic and copies ran while one was open for 1% -> 0% of each run, Pallas kernels for 0% -> 0%
where the time goes in v1:
time: 70.4 us; the launch traced here: 70.2 us
  Pallas kernels  66 us (94%)
  local copies, waits for them, and re-layouts  3.56 us (5%)
    pallas_call x1, Pallas kernels, per_device(): pl.pallas_call(kernel, out_shape=(jax.ShapeDtypeStruct((1, COLS, NY), F32...  66 us
    unnamed x2, local copies, waits for them, and re-layouts  3.56 us

profile of v1, /device:TPU:1, one launch (start us, length us, event | category | flops | bytes accessed | tf_op | source)
XLA Modules:
  0.0 70.2 jit_solution(3356664136171309491)
XLA Ops:
  0.6 66.0 %hybrid_envar.1 = (f32[1,8,1024]{2,1,0:T(8,128)}, bf16[7,8,32,256]{3,2,1,0:T(8,128)(2,1)}) custom-call(s32[2]{0:T(128)} %classes_x.1, s32[8]{0:T(128)} %classes_y.1, bf16[7,8,32,256]{3,2,1,0:T(8,128)(2,1)} %control.1, bf16[7,8,8,1024]{3,2,1,0:T(8,128)(2,1)} %ensemble.1, f32[8,8,1024]{2,1,0:T(8,128)} %innovation.1, f32[8,8,1024]{2,1,0:T(8,128)} %precision.1, ...), custom_call_target="tpu_custom_call" | custom-call | tf_op jit(solution)/shard_map/hybrid_envar/pallas_call | solution.py:262
  66.7 1.4 %copy.12 = f32[1,8,1024]{2,1,0:T(8,128)} copy(f32[1,8,1024]{2,1,0:T(8,128)} %get-tuple-element.4) | data formatting | bytes 65536
  68.0 2.2 %copy.13 = bf16[7,8,32,256]{3,2,1,0:T(8,128)(2,1)} copy(bf16[7,8,32,256]{3,2,1,0:T(8,128)(2,1)} %get-tuple-element.5) | data formatting | bytes 1835008

commit v2 on v1

v2 whole, which is shorter than its diff:
```python
import jax
import jax.numpy as jnp
from jax import lax
from jax.experimental import pallas as pl
from jax.experimental.pallas import tpu as pltpu
from jax.sharding import PartitionSpec as P

MESH = pl.DeviceIdType.MESH
F32 = jnp.float32
BF16 = jnp.bfloat16
NT = (((1,), (1,)), ((), ()))
TN = (((0,), (0,)), ((), ()))

SPACE = 32
LEADER = 2
MEM = 8
XS = 4
M = 7
PAIRS = M // 2
LEVELS = 8
CHUNKS = 4
BATCHES = 4
QUADS = CHUNKS // 2
ROWS = 32
COLS = 8
NX = 256
NY = 1024
B = 128
NB = NY // B
HALF = NY // 2
TILES = 2 * PAIRS + 1
SHARED = PAIRS
FIELD = M * 2 * COLS


def swap_groups(tiles):
    a, b, c, d = tiles
    axis = a.ndim - 1
    lane = lax.broadcasted_iota(jnp.int32, a.shape, axis)
    low = lane < 64
    even = lax.rem(lane, 64) < 32

    def far(p, q):
        return jnp.where(low, p, pltpu.roll(q, 64, axis)), jnp.where(low, pltpu.roll(p, 64, axis), q)

    def near(p, q):
        return jnp.where(even, p, pltpu.roll(q, 32, axis)), jnp.where(even, pltpu.roll(p, 96, axis), q)

    a, c = far(a, c)
    b, d = far(b, d)
    a, b = near(a, b)
    c, d = near(c, d)
    return a, b, c, d


def lanes(t, n=1):
    return slice(t * B, (t + n) * B)


def tiles_forward(c):
    return (0, SHARED + 1) if c % 2 == 0 else (SHARED + 1, TILES)


def tiles_backward(c):
    return (0, SHARED) if c % 2 == 0 else (SHARED, TILES)


def tile_slabs(quad, t):
    if t == SHARED:
        return slice(M - 1, M), slice(4 * quad, 4 * quad + 4)
    half, pair = (0, t) if t < SHARED else (1, t - SHARED - 1)
    first = 4 * quad + 2 * half
    return slice(2 * pair, 2 * pair + 2), slice(first, first + 2)


def kernel(
    classes_x_in, classes_y_in, control, ensemble, innovation, precision, tables_x, tables_y,
    increment, gradient,
    classes_x, classes_y, ctl, ens, inn, prec, tx, ty, wxt, wy, send1, recv1, send2, recv2, field, keep, part, rs_recv, mine, half_send, zrecv,
    total, wres, inc, grad,
    in_sem, out_sem, inc_sem, s1_sem, r1_sem, s2_sem, r2_sem, xs_sem, xr_sem, zs_sem, zr_sem, ws_sem, wr_sem, group_sem, ready_sem,
):
    me = lax.axis_index("space")
    mem = lax.axis_index("mem")
    my_x = lax.rem(mem, XS)
    my_hi = mem // XS
    base = my_hi * XS
    my_level = lax.rem(my_x, 2)
    my_half = my_x // 2
    other_half = lax.rem(mem + XS, MEM)
    across = base + lax.rem(my_x + 2, XS)

    def piece(ref, c):
        return ref.at[2 * c + my_level, :, pl.ds(pl.multiple_of(my_half * HALF, HALF), HALF)]

    loads = []

    def load(src, dst):
        loads.append(pltpu.make_async_copy(src, dst, in_sem.at[len(loads)]))
        loads[-1].start()
        return loads[-1]

    ld_classes = [load(classes_x_in, classes_x), load(classes_y_in, classes_y)]
    ld_tx = load(tables_x, tx)
    ld_ctl = [load(control.at[:, pl.ds(4 * q, 4)], ctl.at[:, pl.ds(4 * q, 4)]) for q in range(QUADS)]
    ld_ty = load(tables_y, ty)
    ld_ens = load(ensemble, ens)
    ld_obs = [load(piece(innovation, c), inn.at[c]) for c in range(CHUNKS)]
    ld_obs += [load(piece(precision, c), prec.at[c]) for c in range(CHUNKS)]

    barrier = pltpu.get_barrier_semaphore()

    @pl.loop(1, SPACE)
    def _(k):
        pl.semaphore_signal(barrier, inc=1, device_id={"space": lax.rem(me + k, SPACE)}, device_id_type=MESH)

    def x_peer(k):
        return lax.rem(my_x + k, XS)

    leads = me == LEADER
    groups = [base + x_peer(k) for k in range(1, XS)] + [other_half]

    @pl.when(leads)
    def _():
        for group in groups:
            pl.semaphore_signal(barrier, inc=1, device_id={"mem": group}, device_id_type=MESH)

    def enter():
        @pl.when(leads)
        def _():
            pl.semaphore_wait(barrier, SPACE - 1 + len(groups))
            for group in groups:
                pl.semaphore_signal(group_sem, inc=1, device_id={"mem": group}, device_id_type=MESH)

        @pl.when(jnp.logical_not(leads))
        def _():
            pl.semaphore_wait(barrier, SPACE - 1)

    def enter_groups():
        @pl.when(leads)
        def _():
            pl.semaphore_wait(group_sem, len(groups))

            @pl.loop(1, SPACE)
            def _(k):
                pl.semaphore_signal(
                    ready_sem, inc=1, device_id={"space": lax.rem(me + k, SPACE)}, device_id_type=MESH
                )

        @pl.when(jnp.logical_not(leads))
        def _():
            pl.semaphore_wait(ready_sem, 1)

    for copy in ld_classes:
        copy.wait()
    ld_tx.wait()
    for b in range(NX // B):
        for j in range(NX // B):
            block = tx[classes_x[b], j - b + 2]
            wxt[lanes(b), lanes(j)] = block.astype(F32).T.astype(BF16)

    def x_filter(c):
        for t in range(*tiles_forward(c)):
            members, levels = tile_slabs(c // 2, t)
            rows = ctl[members, levels].reshape(4 * ROWS, NX)
            out = lax.dot_general(wxt[...], rows, NT, preferred_element_type=F32)
            send1[c // 2, :, :, lanes(t)] = out.reshape(SPACE, COLS, B).astype(BF16)

    def part_of(tiles, c):
        first, last = tiles(c)
        return pl.ds(first * B, (last - first) * B)

    def space_wait(send, recv, tiles, sem, c):
        cut = (c // 2, pl.ds(0, SPACE - 1), slice(None), part_of(tiles, c))
        pltpu.make_async_copy(send.at[cut], recv.at[cut], sem.at[c]).wait()

    def space_start(send, recv, tiles, s_sem, r_sem, c):
        q, cut = c // 2, part_of(tiles, c)

        @pl.loop(1, SPACE)
        def _(k):
            d = lax.rem(me + k, SPACE)
            pltpu.make_async_remote_copy(
                src_ref=send.at[q, d, :, cut], dst_ref=recv.at[q, me, :, cut],
                send_sem=s_sem.at[c], recv_sem=r_sem.at[c],
                device_id={"space": d}, device_id_type=MESH,
            ).start()

        recv[q, me, :, cut] = send[q, me, :, cut]

    def start1(c, batch):
        q, cut = c // 2, part_of(tiles_forward, c)

        @pl.loop(1 if batch == 0 else 0, SPACE // BATCHES)
        def _(t):
            d = lax.rem(me + BATCHES * t + batch, SPACE)
            pltpu.make_async_remote_copy(
                src_ref=send1.at[q, d, :, cut], dst_ref=recv1.at[q, me, :, cut],
                send_sem=s1_sem.at[c, batch], recv_sem=r1_sem.at[c],
                device_id={"space": d}, device_id_type=MESH,
            ).start()

        if batch == 0:
            recv1[q, me, :, cut] = send1[q, me, :, cut]

    def sent1(c, batch):
        n = SPACE // BATCHES - (batch == 0)
        cut = (c // 2, pl.ds(0, n), slice(None), part_of(tiles_forward, c))
        pltpu.make_async_copy(send1.at[cut], recv1.at[cut], s1_sem.at[c, batch]).wait()

    def follow1(c, batch):
        sent1(c - 1, batch)
        start1(c, batch)

    def got1(c):
        space_wait(send1, recv1, tiles_forward, r1_sem, c)

    def start2(c):
        space_start(send2, recv2, tiles_backward, s2_sem, r2_sem, c)

    def sent2(c):
        space_wait(send2, recv2, tiles_backward, s2_sem, c)

    def got2(c):
        space_wait(send2, recv2, tiles_backward, r2_sem, c)

    def band(s):
        return max(0, 2 * s - 2) * B, min(NB, 2 * s + 4) * B

    def to_fields(c):
        q = c // 2
        for t in range(*tiles_forward(c)):
            block = recv1[q, :, :, lanes(t)].astype(F32).reshape(NB, 4, COLS, B)
            out = swap_groups([block[:, j] for j in range(4)])
            for b in range(NB):
                tile = jnp.concatenate([out[i][b] for i in range(4)], axis=0).astype(BF16)
                if t == SHARED:
                    field[c, 2 * PAIRS * 16 :, lanes(b)] = tile[:16]
                    field[c + 1, 2 * PAIRS * 16 :, lanes(b)] = tile[16:]
                else:
                    row = (t if t < SHARED else t - SHARED - 1) * 32
                    field[c, row : row + 32, lanes(b)] = tile

    def member(c, m, cols):
        return ens[m, 2 * c : 2 * c + 2, :, cols].astype(F32).reshape(2 * COLS, -1)

    def forward(c):
        to_fields(c)
        for s in range(NB // 2):
            lo, hi = band(s)
            cols = lanes(2 * s, 2)
            out = jnp.dot(field[c, :, lo:hi], wy[lo:hi, cols], preferred_element_type=F32)
            acc = member(c, 0, cols) * out[:16]
            for m in range(1, M):
                acc = acc + member(c, m, cols) * out[16 * m : 16 * (m + 1)]
            for level in range(2):
                part[c, 2 * (s // 2) + level, :, lanes(2 * (s % 2), 2)] = acc[COLS * level : COLS * (level + 1)]
        for k in range(1, XS):
            p = x_peer(k)
            pltpu.make_async_remote_copy(
                src_ref=part.at[c, p], dst_ref=rs_recv.at[c, my_x], send_sem=xs_sem.at[c], recv_sem=xr_sem.at[c],
                device_id={"mem": base + p}, device_id_type=MESH,
            ).start()
        rs_recv[c, my_x] = part[c, my_x]

    def peers_wait(ref, sem, c):
        cut = (c, pl.ds(0, XS - 1))
        pltpu.make_async_copy(ref.at[cut], ref.at[cut], sem.at[c]).wait()

    def half_copy(c):
        return pltpu.make_async_remote_copy(
            src_ref=half_send.at[c], dst_ref=zrecv.at[c], send_sem=zs_sem.at[c], recv_sem=zr_sem.at[c],
            device_id={"mem": other_half}, device_id_type=MESH,
        )

    def sum_x(c):
        peers_wait(rs_recv, xr_sem, c)
        mine[c] = (rs_recv[c, 0] + rs_recv[c, 1]) + (rs_recv[c, 2] + rs_recv[c, 3])
        half_send[c] = mine[c].astype(BF16)
        half_copy(c).start()

    def weigh(c):
        half_copy(c).wait_recv()
        total[c] = mine[c] + zrecv[c].astype(F32)
        wres[c, my_x] = (prec[c] * (total[c] - inn[c])).astype(BF16)
        for k in range(1, XS):
            pltpu.make_async_remote_copy(
                src_ref=wres.at[c, my_x], dst_ref=wres.at[c, my_x], send_sem=ws_sem.at[c], recv_sem=wr_sem.at[c],
                device_id={"mem": base + x_peer(k)}, device_id_type=MESH,
            ).start()

    def backward(c):
        q, odd = c // 2, c % 2
        peers_wait(wres, wr_sem, c)
        weight = jnp.concatenate(
            [
                jnp.concatenate([wres[c, level].astype(F32), wres[c, 2 + level].astype(F32)], axis=1)
                for level in range(2)
            ],
            axis=0,
        )
        for m in range(M):
            field[c, 16 * m : 16 * (m + 1)] = (member(c, m, slice(None)) * weight).astype(BF16)
        for s in range(NB // 2):
            lo, hi = band(s)
            out = lax.dot_general(field[c, :, lo:hi], wy[lanes(2 * s, 2), lo:hi], NT, preferred_element_type=F32)
            for b in (2 * s, 2 * s + 1):
                cols = lanes(b - 2 * s)
                groups = [
                    (pair + odd * (SHARED + 1), out[32 * pair : 32 * (pair + 1), cols]) for pair in range(PAIRS)
                ]
                last = out[32 * PAIRS :, cols]
                if odd:
                    groups.append((SHARED, jnp.concatenate([keep[:, lanes(b)], last], axis=0)))
                else:
                    keep[:, lanes(b)] = last
                for t, rows in groups:
                    rows = rows.reshape(4, COLS, B)
                    swapped = swap_groups([rows[i] for i in range(4)])
                    for j in range(4):
                        send2[q, 4 * b + j, :, lanes(t)] = swapped[j].astype(BF16)
        start2(c)

    def out_copies(c):
        pairs = (slice(0, 2 * PAIRS), slice(2 * c, 2 * c + 2))
        copies = [pltpu.make_async_copy(grad.at[pairs], gradient.at[pairs], out_sem.at[c])]
        if c % 2:
            last = (slice(M - 1, M), slice(2 * c - 2, 2 * c + 2))
            copies.append(pltpu.make_async_copy(grad.at[last], gradient.at[last], out_sem.at[CHUNKS + c // 2]))
        return copies

    def finish(c):
        got2(c)
        for t in range(*tiles_backward(c)):
            slabs = tile_slabs(c // 2, t)
            cols = recv2[c // 2, :, :, lanes(t)].astype(F32).reshape(NX, B).astype(BF16)
            out = lax.dot_general(cols, wxt[...], TN, preferred_element_type=F32)
            old = ctl[slabs]
            grad[slabs] = (old.astype(F32) + out.reshape(old.shape)).astype(BF16)
        for copy in out_copies(c):
            copy.start()

    ld_ctl[0].wait()
    x_filter(0)
    enter()
    for batch in range(BATCHES):
        start1(0, batch)
    x_filter(1)
    ld_ctl[1].wait()
    follow1(1, 0)
    x_filter(2)
    follow1(1, 1)
    x_filter(3)
    enter_groups()

    ld_ty.wait()
    for b in range(NB):
        for j in range(NB):
            if abs(j - b) <= 2:
                wy[lanes(j), lanes(b)] = ty[classes_y[b], j - b + 2]
            elif abs(j - b) == 3:
                wy[lanes(j), lanes(b)] = jnp.zeros((B, B), BF16)
    ld_ens.wait()
    for copy in ld_obs:
        copy.wait()

    follow1(1, 2)
    follow1(1, 3)
    got1(0)
    forward(0)
    for batch in range(BATCHES):
        follow1(2, batch)
    got1(1)
    forward(1)
    sum_x(0)
    for batch in range(BATCHES):
        follow1(3, batch)
    got1(2)
    forward(2)
    sum_x(1)
    weigh(0)
    got1(3)
    forward(3)
    sum_x(2)
    backward(0)
    weigh(1)
    sum_x(3)
    backward(1)
    weigh(2)
    backward(2)
    weigh(3)

    kept = pl.ds(pl.multiple_of(my_half * HALF, HALF), HALF)
    inc[0, :, kept] = total[2 * my_hi + my_half]
    given = pltpu.make_async_remote_copy(
        src_ref=total.at[2 * my_hi + 1 - my_half], dst_ref=inc.at[0, :, kept],
        send_sem=inc_sem.at[0], recv_sem=inc_sem.at[1], device_id={"mem": across}, device_id_type=MESH,
    )
    given.start()
    backward(3)
    finish(0)
    finish(1)
    given.wait()
    inc_copy = pltpu.make_async_copy(inc, increment, out_sem.at[CHUNKS + QUADS])
    inc_copy.start()
    finish(2)
    for c in range(CHUNKS):
        peers_wait(rs_recv, xs_sem, c)
        half_copy(c).wait_send()
        peers_wait(wres, ws_sem, c)
        sent2(c)
    for batch in range(BATCHES):
        sent1(CHUNKS - 1, batch)
    finish(3)
    inc_copy.wait()
    for c in range(CHUNKS):
        for copy in out_copies(c):
            copy.wait()


def per_device(control, ensemble, innovation, precision_obs, classes_x, classes_y, tables_x, tables_y):
    any_space = pl.BlockSpec(memory_space=pl.ANY)
    dma = pltpu.SemaphoreType.DMA
    message = pltpu.VMEM((QUADS, SPACE, COLS, TILES * B), BF16)
    sums = pltpu.VMEM((CHUNKS, XS, COLS, HALF), F32)
    piece = pltpu.VMEM((CHUNKS, COLS, HALF), F32)
    return pl.pallas_call(
        kernel,
        out_shape=(
            jax.ShapeDtypeStruct((1, COLS, NY), F32),
            jax.ShapeDtypeStruct((M, LEVELS, ROWS, NX), BF16),
        ),
        in_specs=[any_space] * 8,
        out_specs=(any_space, any_space),
        scratch_shapes=[
            pltpu.SMEM(classes_x.shape, jnp.int32),
            pltpu.SMEM(classes_y.shape, jnp.int32),
            pltpu.VMEM((M, LEVELS, ROWS, NX), BF16),
            pltpu.VMEM((M, LEVELS, COLS, NY), BF16),
            piece,
            piece,
            pltpu.VMEM(tables_x.shape, BF16),
            pltpu.VMEM(tables_y.shape, BF16),
            pltpu.VMEM((NX, NX), BF16),
            pltpu.VMEM((NY, NY), BF16),
            message,
            message,
            message,
            message,
            pltpu.VMEM((CHUNKS, FIELD, NY), BF16),
            pltpu.VMEM((2 * COLS, NY), F32),
            sums,
            sums,
            piece,
            pltpu.VMEM((CHUNKS, COLS, HALF), BF16),
            pltpu.VMEM((CHUNKS, COLS, HALF), BF16),
            piece,
            pltpu.VMEM((CHUNKS, XS, COLS, HALF), BF16),
            pltpu.VMEM((1, COLS, NY), F32),
            pltpu.VMEM((M, LEVELS, ROWS, NX), BF16),
            dma((7 + 2 * CHUNKS,)),
            dma((CHUNKS + QUADS + 1,)),
            dma((2,)),
        ]
        + [dma((CHUNKS, BATCHES))]
        + [dma((CHUNKS,))] * 9
        + [pltpu.SemaphoreType.REGULAR] * 2,
        compiler_params=pltpu.CompilerParams(
            collective_id=0, has_side_effects=True, vmem_limit_bytes=63 << 20
        ),
        name="hybrid_envar",
    )(classes_x, classes_y, control, ensemble, innovation, precision_obs, tables_x, tables_y)


def solution(mesh):
    in_specs = (
        P("mem", None, "space", None),
        P("mem", None, "space", None),
        P(None, "space", None),
        P(None, "space", None),
        P(),
        P(),
        P(),
        P(),
    )
    out_specs = (P("mem", "space", None), P("mem", None, "space", None))
    return jax.shard_map(
        per_device, mesh=mesh, in_specs=in_specs, out_specs=out_specs, check_vma=False
    )
```

time: 70.4 us -> 62.1 us (0.88)
  Pallas kernels: 66 us -> 57.7 us
    pallas_call x1, Pallas kernels: 66 us -> 57.7 us  [per_device(): pl.pallas_call(kernel, out_shape=(jax.ShapeDtypeStruct((1, COLS, NY), F32...]
where the time goes in v2:
time: 62.1 us; the launch traced here: 61.9 us
  Pallas kernels  57.7 us (93%)
  local copies, waits for them, and re-layouts  3.56 us (6%)
  between operations  0.64 us (1%)
    pallas_call x1, Pallas kernels, per_device(): pl.pallas_call(kernel, out_shape=(jax.ShapeDtypeStruct((1, COLS, NY), F32...  57.7 us
    unnamed x2, local copies, waits for them, and re-layouts  3.56 us

profile of v2, /device:TPU:1, one launch (start us, length us, event | category | flops | bytes accessed | tf_op | source)
XLA Modules:
  0.0 61.9 jit_solution(3957129173550435578)
XLA Ops:
  0.6 57.7 %hybrid_envar.1 = (f32[1,8,1024]{2,1,0:T(8,128)}, bf16[7,8,32,256]{3,2,1,0:T(8,128)(2,1)}) custom-call(s32[2]{0:T(128)} %classes_x_in.1, s32[8]{0:T(128)} %classes_y_in.1, bf16[7,8,32,256]{3,2,1,0:T(8,128)(2,1)} %control.1, bf16[7,8,8,1024]{3,2,1,0:T(8,128)(2,1)} %ensemble.1, f32[8,8,1024]{2,1,0:T(8,128)} %innovation.1, f32[8,8,1024]{2,1,0:T(8,128)} %precision.1, ...), custom_call_target="tpu_custom_call" | custom-call | tf_op jit(solution)/shard_map/hybrid_envar/pallas_call | solution.py:427
  58.4 1.4 %copy.12 = f32[1,8,1024]{2,1,0:T(8,128)} copy(f32[1,8,1024]{2,1,0:T(8,128)} %get-tuple-element.4) | data formatting | bytes 65536
  59.8 2.2 %copy.13 = bf16[7,8,32,256]{3,2,1,0:T(8,128)(2,1)} copy(bf16[7,8,32,256]{3,2,1,0:T(8,128)(2,1)} %get-tuple-element.5) | data formatting | bytes 1835008

commit v3 on v2

--- a/solution.py
+++ b/solution.py
@@ -97,7 +97,6 @@
 
     def load(src, dst):
         loads.append(pltpu.make_async_copy(src, dst, in_sem.at[len(loads)]))
-        loads[-1].start()
         return loads[-1]
 
     ld_classes = [load(classes_x_in, classes_x), load(classes_y_in, classes_y)]
@@ -107,6 +106,10 @@
     ld_ens = load(ensemble, ens)
     ld_obs = [load(piece(innovation, c), inn.at[c]) for c in range(CHUNKS)]
     ld_obs += [load(piece(precision, c), prec.at[c]) for c in range(CHUNKS)]
+
+    urgent = ld_classes + [ld_tx, ld_ctl[0]]
+    for copy in urgent:
+        copy.start()
 
     barrier = pltpu.get_barrier_semaphore()
 
@@ -341,6 +344,9 @@
             copy.start()
 
     ld_ctl[0].wait()
+    for copy in loads:
+        if all(copy is not other for other in urgent):
+            copy.start()
     x_filter(0)
     enter()
     for batch in range(BATCHES):
@@ -418,18 +424,32 @@
             copy.wait()
 
 
+def write_out(inc_in, grad_in, increment, gradient, inc, grad, sem):
+    copies = [(inc_in, inc, increment)] + [(grad_in.at[m], grad.at[m], gradient.at[m]) for m in range(M)]
+    loads = [pltpu.make_async_copy(src, via, sem.at[0, n]) for n, (src, via, _) in enumerate(copies)]
+    stores = [pltpu.make_async_copy(via, dst, sem.at[1, n]) for n, (_, via, dst) in enumerate(copies)]
+    for load in loads:
+        load.start()
+    for load, store in zip(loads, stores):
+        load.wait()
+        store.start()
+    for store in stores:
+        store.wait()
+
+
 def per_device(control, ensemble, innovation, precision_obs, classes_x, classes_y, tables_x, tables_y):
     any_space = pl.BlockSpec(memory_space=pl.ANY)
     dma = pltpu.SemaphoreType.DMA
     message = pltpu.VMEM((QUADS, SPACE, COLS, TILES * B), BF16)
     sums = pltpu.VMEM((CHUNKS, XS, COLS, HALF), F32)
     piece = pltpu.VMEM((CHUNKS, COLS, HALF), F32)
-    return pl.pallas_call(
+    shapes = (
+        jax.ShapeDtypeStruct((1, COLS, NY), F32),
+        jax.ShapeDtypeStruct((M, LEVELS, ROWS, NX), BF16),
+    )
+    results = pl.pallas_call(
         kernel,
-        out_shape=(
-            jax.ShapeDtypeStruct((1, COLS, NY), F32),
-            jax.ShapeDtypeStruct((M, LEVELS, ROWS, NX), BF16),
-        ),
+        out_shape=shapes,
         in_specs=[any_space] * 8,
         out_specs=(any_space, any_space),
         scratch_shapes=[
@@ -470,6 +490,15 @@
         ),
         name="hybrid_envar",
     )(classes_x, classes_y, control, ensemble, innovation, precision_obs, tables_x, tables_y)
+    return pl.pallas_call(
+        write_out,
+        out_shape=shapes,
+        in_specs=[any_space] * 2,
+        out_specs=(any_space,) * 2,
+        scratch_shapes=[pltpu.VMEM(shape.shape, shape.dtype) for shape in shapes] + [dma((2, M + 1))],
+        compiler_params=pltpu.CompilerParams(vmem_limit_bytes=63 << 20),
+        name="write_out",
+    )(*results)
 
 
 def solution(mesh):

time: 62.1 us -> 60.6 us (0.976)
  local copies, waits for them, and re-layouts: 3.56 us -> 0 us
  Pallas kernels: 57.7 us -> 59.8 us
    unnamed x2 -> x0, local copies, waits for them, and re-layouts: 3.56 us -> none
    pallas_call x1 -> x2, Pallas kernels: 57.7 us -> 59.8 us  [the longest x1 57.7 us: per_device(): pl.pallas_call(kernel, out_shape=shapes, in_specs=[any_space] * 8, out_sp...]
where the time goes in v3:
time: 60.6 us; the launch traced here: 60.4 us
  Pallas kernels  59.8 us (99%)
  between operations  0.64 us (1%)
    pallas_call x1, Pallas kernels, per_device(): pl.pallas_call(kernel, out_shape=shapes, in_specs=[any_space] * 8, out_sp...  57.7 us
    pallas_call x1, Pallas kernels, per_device(): pl.pallas_call(write_out, out_shape=shapes, in_specs=[any_space] * 2, out...  2.06 us

profile of v3, /device:TPU:1, one launch (start us, length us, event | category | flops | bytes accessed | tf_op | source)
XLA Modules:
  0.0 60.4 jit_solution(18059135669107759272)
XLA Ops:
  0.6 57.7 %hybrid_envar.1 = (f32[1,8,1024]{2,1,0:T(8,128)}, bf16[7,8,32,256]{3,2,1,0:T(8,128)(2,1)}) custom-call(s32[2]{0:T(128)} %classes_x_in.1, s32[8]{0:T(128)} %classes_y_in.1, bf16[7,8,32,256]{3,2,1,0:T(8,128)(2,1)} %control.1, bf16[7,8,8,1024]{3,2,1,0:T(8,128)(2,1)} %ensemble.1, f32[8,8,1024]{2,1,0:T(8,128)} %innovation.1, f32[8,8,1024]{2,1,0:T(8,128)} %precision.1, ...), custom_call_target="tpu_custom_call" | custom-call | tf_op jit(solution)/shard_map/hybrid_envar/pallas_call | solution.py:450
  58.4 2.1 %write_out.1 = (f32[1,8,1024]{2,1,0:T(8,128)}, bf16[7,8,32,256]{3,2,1,0:T(8,128)(2,1)}) custom-call(f32[1,8,1024]{2,1,0:T(8,128)} %get-tuple-element.4.inc_in, bf16[7,8,32,256]{3,2,1,0:T(8,128)(2,1)} %get-tuple-element.5.grad_in), custom_call_target="tpu_custom_call" | custom-call | tf_op jit(solution)/shard_map/write_out/pallas_call | solution.py:493

commit v4 on v3

--- a/solution.py
+++ b/solution.py
@@ -18,6 +18,7 @@
 M = 7
 PAIRS = M // 2
 LEVELS = 8
+CLASSES = 8
 CHUNKS = 4
 BATCHES = 4
 QUADS = CHUNKS // 2
@@ -75,10 +76,10 @@
 
 def kernel(
     classes_x_in, classes_y_in, control, ensemble, innovation, precision, tables_x, tables_y,
-    increment, gradient,
+    increment, gradient, last, wxt_out,
     classes_x, classes_y, ctl, ens, inn, prec, tx, ty, wxt, wy, send1, recv1, send2, recv2, field, keep, part, rs_recv, mine, half_send, zrecv,
     total, wres, inc, grad,
-    in_sem, out_sem, inc_sem, s1_sem, r1_sem, s2_sem, r2_sem, xs_sem, xr_sem, zs_sem, zr_sem, ws_sem, wr_sem, group_sem, ready_sem,
+    in_sem, out_sem, inc_sem, s1_sem, r1_sem, s2_sem, r2_sem, xs_sem, xr_sem, zs_sem, zr_sem, ws_sem, wr_sem, last_sem, group_sem, ready_sem,
 ):
     me = lax.axis_index("space")
     mem = lax.axis_index("mem")
@@ -95,21 +96,32 @@
 
     loads = []
 
-    def load(src, dst):
-        loads.append(pltpu.make_async_copy(src, dst, in_sem.at[len(loads)]))
+    def load(src, dst, pieces=1):
+        sem = in_sem.at[len(loads)]
+        size = src.shape[0] // pieces
+        cuts = [pl.ds(n * size, size) for n in range(pieces)]
+        parts = [pltpu.make_async_copy(src.at[cut], dst.at[cut], sem) for cut in cuts]
+        loads.append((parts, pltpu.make_async_copy(src, dst, sem)))
         return loads[-1]
 
+    def begin(load):
+        for part in load[0]:
+            part.start()
+
+    def end(load):
+        load[1].wait()
+
     ld_classes = [load(classes_x_in, classes_x), load(classes_y_in, classes_y)]
-    ld_tx = load(tables_x, tx)
-    ld_ctl = [load(control.at[:, pl.ds(4 * q, 4)], ctl.at[:, pl.ds(4 * q, 4)]) for q in range(QUADS)]
-    ld_ty = load(tables_y, ty)
-    ld_ens = load(ensemble, ens)
+    ld_tx = load(tables_x, tx, CLASSES)
+    ld_ctl = [load(control.at[:, pl.ds(4 * q, 4)], ctl.at[:, pl.ds(4 * q, 4)], M) for q in range(QUADS)]
+    ld_ty = load(tables_y, ty, CLASSES)
+    ld_ens = load(ensemble, ens, M)
     ld_obs = [load(piece(innovation, c), inn.at[c]) for c in range(CHUNKS)]
     ld_obs += [load(piece(precision, c), prec.at[c]) for c in range(CHUNKS)]
 
     urgent = ld_classes + [ld_tx, ld_ctl[0]]
-    for copy in urgent:
-        copy.start()
+    for item in urgent:
+        begin(item)
 
     barrier = pltpu.get_barrier_semaphore()
 
@@ -154,13 +166,15 @@
         def _():
             pl.semaphore_wait(ready_sem, 1)
 
-    for copy in ld_classes:
-        copy.wait()
-    ld_tx.wait()
+    for item in ld_classes:
+        end(item)
+    end(ld_tx)
     for b in range(NX // B):
         for j in range(NX // B):
             block = tx[classes_x[b], j - b + 2]
             wxt[lanes(b), lanes(j)] = block.astype(F32).T.astype(BF16)
+    wxt_copy = pltpu.make_async_copy(wxt, wxt_out, last_sem.at[0])
+    wxt_copy.start()
 
     def x_filter(c):
         for t in range(*tiles_forward(c)):
@@ -177,19 +191,26 @@
         cut = (c // 2, pl.ds(0, SPACE - 1), slice(None), part_of(tiles, c))
         pltpu.make_async_copy(send.at[cut], recv.at[cut], sem.at[c]).wait()
 
-    def space_start(send, recv, tiles, s_sem, r_sem, c):
-        q, cut = c // 2, part_of(tiles, c)
+    own_cut = (QUADS - 1, me, slice(None), part_of(tiles_backward, CHUNKS - 1))
+    own_copy = pltpu.make_async_copy(send2.at[own_cut], last.at[me], last_sem.at[1])
+
+    def start2(c):
+        q, cut = c // 2, part_of(tiles_backward, c)
 
         @pl.loop(1, SPACE)
         def _(k):
             d = lax.rem(me + k, SPACE)
             pltpu.make_async_remote_copy(
-                src_ref=send.at[q, d, :, cut], dst_ref=recv.at[q, me, :, cut],
-                send_sem=s_sem.at[c], recv_sem=r_sem.at[c],
+                src_ref=send2.at[q, d, :, cut],
+                dst_ref=last.at[me] if c == CHUNKS - 1 else recv2.at[q, me, :, cut],
+                send_sem=s2_sem.at[c], recv_sem=r2_sem.at[c],
                 device_id={"space": d}, device_id_type=MESH,
             ).start()
 
-        recv[q, me, :, cut] = send[q, me, :, cut]
+        if c == CHUNKS - 1:
+            own_copy.start()
+        else:
+            recv2[q, me, :, cut] = send2[q, me, :, cut]
 
     def start1(c, batch):
         q, cut = c // 2, part_of(tiles_forward, c)
@@ -218,14 +239,15 @@
     def got1(c):
         space_wait(send1, recv1, tiles_forward, r1_sem, c)
 
-    def start2(c):
-        space_start(send2, recv2, tiles_backward, s2_sem, r2_sem, c)
-
     def sent2(c):
         space_wait(send2, recv2, tiles_backward, s2_sem, c)
 
     def got2(c):
-        space_wait(send2, recv2, tiles_backward, r2_sem, c)
+        if c == CHUNKS - 1:
+            cut = pl.ds(0, SPACE - 1)
+            pltpu.make_async_copy(last.at[cut], last.at[cut], r2_sem.at[c]).wait()
+        else:
+            space_wait(send2, recv2, tiles_backward, r2_sem, c)
 
     def band(s):
         return max(0, 2 * s - 2) * B, min(NB, 2 * s + 4) * B
@@ -328,8 +350,8 @@
         pairs = (slice(0, 2 * PAIRS), slice(2 * c, 2 * c + 2))
         copies = [pltpu.make_async_copy(grad.at[pairs], gradient.at[pairs], out_sem.at[c])]
         if c % 2:
-            last = (slice(M - 1, M), slice(2 * c - 2, 2 * c + 2))
-            copies.append(pltpu.make_async_copy(grad.at[last], gradient.at[last], out_sem.at[CHUNKS + c // 2]))
+            shared = (slice(M - 1, M), slice(2 * c - 2, 2 * c + 2))
+            copies.append(pltpu.make_async_copy(grad.at[shared], gradient.at[shared], out_sem.at[CHUNKS + c // 2]))
         return copies
 
     def finish(c):
@@ -343,32 +365,32 @@
         for copy in out_copies(c):
             copy.start()
 
-    ld_ctl[0].wait()
-    for copy in loads:
-        if all(copy is not other for other in urgent):
-            copy.start()
+    end(ld_ctl[0])
+    for item in loads:
+        if all(item is not other for other in urgent):
+            begin(item)
     x_filter(0)
     enter()
     for batch in range(BATCHES):
         start1(0, batch)
     x_filter(1)
-    ld_ctl[1].wait()
+    end(ld_ctl[1])
     follow1(1, 0)
     x_filter(2)
     follow1(1, 1)
     x_filter(3)
     enter_groups()
 
-    ld_ty.wait()
+    end(ld_ty)
     for b in range(NB):
         for j in range(NB):
             if abs(j - b) <= 2:
                 wy[lanes(j), lanes(b)] = ty[classes_y[b], j - b + 2]
             elif abs(j - b) == 3:
                 wy[lanes(j), lanes(b)] = jnp.zeros((B, B), BF16)
-    ld_ens.wait()
-    for copy in ld_obs:
-        copy.wait()
+    end(ld_ens)
+    for item in ld_obs:
+        end(item)
 
     follow1(1, 2)
     follow1(1, 3)
@@ -417,22 +439,44 @@
         sent2(c)
     for batch in range(BATCHES):
         sent1(CHUNKS - 1, batch)
-    finish(3)
+    own_copy.wait()
+    wxt_copy.wait()
     inc_copy.wait()
-    for c in range(CHUNKS):
+    for c in range(CHUNKS - 1):
         for copy in out_copies(c):
             copy.wait()
-
-
-def write_out(inc_in, grad_in, increment, gradient, inc, grad, sem):
-    copies = [(inc_in, inc, increment)] + [(grad_in.at[m], grad.at[m], gradient.at[m]) for m in range(M)]
+    got2(CHUNKS - 1)
+
+
+def write_out(inc_in, grad_in, last_in, wxt_in, control, increment, gradient, inc, grad, last, wxt, ctl, sem):
+    pairs = (slice(0, 2 * PAIRS), slice(LEVELS - 2, LEVELS))
+    shared = (slice(M - 1, M), slice(LEVELS - 4, LEVELS))
+    needs = [
+        pltpu.make_async_copy(last_in, last, sem.at[2, 0]),
+        pltpu.make_async_copy(wxt_in, wxt, sem.at[2, 1]),
+        pltpu.make_async_copy(control.at[pairs], ctl.at[pairs], sem.at[2, 2]),
+        pltpu.make_async_copy(control.at[shared], ctl.at[shared], sem.at[2, 3]),
+    ]
+    cuts = [(m, slice(0, LEVELS - 4 if m == M - 1 else LEVELS - 2)) for m in range(M)]
+    copies = [(inc_in, inc, increment)] + [(grad_in.at[cut], grad.at[cut], gradient.at[cut]) for cut in cuts]
     loads = [pltpu.make_async_copy(src, via, sem.at[0, n]) for n, (src, via, _) in enumerate(copies)]
     stores = [pltpu.make_async_copy(via, dst, sem.at[1, n]) for n, (_, via, dst) in enumerate(copies)]
-    for load in loads:
-        load.start()
-    for load, store in zip(loads, stores):
+    for copy in needs + loads:
+        copy.start()
+    for copy in needs:
+        copy.wait()
+    for t in range(SHARED, TILES):
+        slabs = tile_slabs(QUADS - 1, t)
+        cols = last[:, :, lanes(t - SHARED)].astype(F32).reshape(NX, B).astype(BF16)
+        out = lax.dot_general(cols, wxt[...], TN, preferred_element_type=F32)
+        old = ctl[slabs]
+        grad[slabs] = (old.astype(F32) + out.reshape(old.shape)).astype(BF16)
+        ends = pltpu.make_async_copy(grad.at[slabs], gradient.at[slabs], sem.at[3, t - SHARED])
+        ends.start()
+        stores.append(ends)
+    for n, load in enumerate(loads):
         load.wait()
-        store.start()
+        stores[n].start()
     for store in stores:
         store.wait()
 
@@ -449,9 +493,13 @@
     )
     results = pl.pallas_call(
         kernel,
-        out_shape=shapes,
+        out_shape=shapes
+        + (
+            jax.ShapeDtypeStruct((SPACE, COLS, (TILES - SHARED) * B), BF16),
+            jax.ShapeDtypeStruct((NX, NX), BF16),
+        ),
         in_specs=[any_space] * 8,
-        out_specs=(any_space, any_space),
+        out_specs=(any_space,) * 4,
         scratch_shapes=[
             pltpu.SMEM(classes_x.shape, jnp.int32),
             pltpu.SMEM(classes_y.shape, jnp.int32),
@@ -484,6 +532,7 @@
         ]
         + [dma((CHUNKS, BATCHES))]
         + [dma((CHUNKS,))] * 9
+        + [dma((2,))]
         + [pltpu.SemaphoreType.REGULAR] * 2,
         compiler_params=pltpu.CompilerParams(
             collective_id=0, has_side_effects=True, vmem_limit_bytes=63 << 20
@@ -493,12 +542,18 @@
     return pl.pallas_call(
         write_out,
         out_shape=shapes,
-        in_specs=[any_space] * 2,
+        in_specs=[any_space] * 5,
         out_specs=(any_space,) * 2,
-        scratch_shapes=[pltpu.VMEM(shape.shape, shape.dtype) for shape in shapes] + [dma((2, M + 1))],
+        scratch_shapes=[pltpu.VMEM(shape.shape, shape.dtype) for shape in shapes]
+        + [
+            pltpu.VMEM((SPACE, COLS, (TILES - SHARED) * B), BF16),
+            pltpu.VMEM((NX, NX), BF16),
+            pltpu.VMEM((M, LEVELS, ROWS, NX), BF16),
+            dma((4, M + 1)),
+        ],
         compiler_params=pltpu.CompilerParams(vmem_limit_bytes=63 << 20),
         name="write_out",
-    )(*results)
+    )(*results, control)
 
 
 def solution(mesh):

time: 60.6 us -> 60.2 us (level)
  no operation moved by 1% of the time
where the time goes in v4:
time: 60.2 us; the launch traced here: 60 us
  Pallas kernels  59.4 us (99%)
  between operations  0.64 us (1%)
    pallas_call x1, Pallas kernels, per_device(): pl.pallas_call(kernel, out_shape=shapes + (jax.ShapeDtypeStruct((SPACE, C...  56.9 us
    pallas_call x1, Pallas kernels, per_device(): pl.pallas_call(write_out, out_shape=shapes, in_specs=[any_space] * 5, out...  2.5 us

profile of v4, /device:TPU:1, one launch (start us, length us, event | category | flops | bytes accessed | tf_op | source)
XLA Modules:
  0.0 60.0 jit_solution(17969987418559926680)
XLA Ops:
  0.6 56.9 %hybrid_envar.1 = (f32[1,8,1024]{2,1,0:T(8,128)}, bf16[7,8,32,256]{3,2,1,0:T(8,128)(2,1)}, bf16[32,8,512]{2,1,0:T(8,128)(2,1)}, bf16[256,256]{1,0:T(8,128)(2,1)}) custom-call(s32[2]{0:T(128)} %classes_x_in.1, s32[8]{0:T(128)} %classes_y_in.1, bf16[7,8,32,256]{3,2,1,0:T(8,128)(2,1)} %control.3, bf16[7,8,8,1024]{3,2,1,0:T(8,128)(2,1)} %ensemble.1, ...), custom_call_target="tpu_custom_call" | custom-call | tf_op jit(solution)/shard_map/hybrid_envar/pallas_call | solution.py:494
  57.5 2.5 %write_out.1 = (f32[1,8,1024]{2,1,0:T(8,128)}, bf16[7,8,32,256]{3,2,1,0:T(8,128)(2,1)}) custom-call(f32[1,8,1024]{2,1,0:T(8,128)} %get-tuple-element.6.inc_in, bf16[7,8,32,256]{3,2,1,0:T(8,128)(2,1)} %get-tuple-element.7.grad_in, bf16[32,8,512]{2,1,0:T(8,128)(2,1)} %get-tuple-element.8.last_in, bf16[256,256]{1,0:T(8,128)(2,1)} %get-tuple-element.9.wxt_in, ...), custom_call_target="tpu_custom_call" | custom-call | tf_op jit(solution)/shard_map/write_out/pallas_call | solution.py:542

commit v5 on v4

--- a/solution.py
+++ b/solution.py
@@ -119,10 +119,6 @@
     ld_obs = [load(piece(innovation, c), inn.at[c]) for c in range(CHUNKS)]
     ld_obs += [load(piece(precision, c), prec.at[c]) for c in range(CHUNKS)]
 
-    urgent = ld_classes + [ld_tx, ld_ctl[0]]
-    for item in urgent:
-        begin(item)
-
     barrier = pltpu.get_barrier_semaphore()
 
     @pl.loop(1, SPACE)
@@ -139,6 +135,10 @@
     def _():
         for group in groups:
             pl.semaphore_signal(barrier, inc=1, device_id={"mem": group}, device_id_type=MESH)
+
+    urgent = ld_classes + [ld_tx, ld_ctl[0]]
+    for item in urgent:
+        begin(item)
 
     def enter():
         @pl.when(leads)
@@ -411,11 +411,12 @@
     forward(3)
     sum_x(2)
     backward(0)
+    sum_x(3)
     weigh(1)
-    sum_x(3)
     backward(1)
     weigh(2)
     backward(2)
+    finish(0)
     weigh(3)
 
     kept = pl.ds(pl.multiple_of(my_half * HALF, HALF), HALF)
@@ -426,7 +427,6 @@
     )
     given.start()
     backward(3)
-    finish(0)
     finish(1)
     given.wait()
     inc_copy = pltpu.make_async_copy(inc, increment, out_sem.at[CHUNKS + QUADS])

time: 60.2 us -> 60.4 us (level)
  no operation moved by 1% of the time
where the time goes in v5:
time: 60.4 us; the launch traced here: 60.2 us
  Pallas kernels  59.6 us (99%)
  between operations  0.64 us (1%)
    pallas_call x1, Pallas kernels, per_device(): pl.pallas_call(kernel, out_shape=shapes + (jax.ShapeDtypeStruct((SPACE, C...  57.1 us
    pallas_call x1, Pallas kernels, per_device(): pl.pallas_call(write_out, out_shape=shapes, in_specs=[any_space] * 5, out...  2.5 us

profile of v5, /device:TPU:1, one launch (start us, length us, event | category | flops | bytes accessed | tf_op | source)
XLA Modules:
  0.0 60.2 jit_solution(10227775691611074604)
XLA Ops:
  0.6 57.1 %hybrid_envar.1 = (f32[1,8,1024]{2,1,0:T(8,128)}, bf16[7,8,32,256]{3,2,1,0:T(8,128)(2,1)}, bf16[32,8,512]{2,1,0:T(8,128)(2,1)}, bf16[256,256]{1,0:T(8,128)(2,1)}) custom-call(s32[2]{0:T(128)} %classes_x_in.1, s32[8]{0:T(128)} %classes_y_in.1, bf16[7,8,32,256]{3,2,1,0:T(8,128)(2,1)} %control.3, bf16[7,8,8,1024]{3,2,1,0:T(8,128)(2,1)} %ensemble.1, ...), custom_call_target="tpu_custom_call" | custom-call | tf_op jit(solution)/shard_map/hybrid_envar/pallas_call | solution.py:494
  57.7 2.5 %write_out.1 = (f32[1,8,1024]{2,1,0:T(8,128)}, bf16[7,8,32,256]{3,2,1,0:T(8,128)(2,1)}) custom-call(f32[1,8,1024]{2,1,0:T(8,128)} %get-tuple-element.6.inc_in, bf16[7,8,32,256]{3,2,1,0:T(8,128)(2,1)} %get-tuple-element.7.grad_in, bf16[32,8,512]{2,1,0:T(8,128)(2,1)} %get-tuple-element.8.last_in, bf16[256,256]{1,0:T(8,128)(2,1)} %get-tuple-element.9.wxt_in, ...), custom_call_target="tpu_custom_call" | custom-call | tf_op jit(solution)/shard_map/write_out/pallas_call | solution.py:542
